TPU v7x, 32 devices: a whole 2x2x4 slice. The times are simulated.
32 devices in a mesh: mob: 2 (over x), imm: 16 (over z, y, core).
Axes of the slice: x: 2, y: 2, z: 4, core: 2. Of those that a mesh axis runs over, the one named last changes fastest.
Arguments:
- mobile_positions: float32 [512, 3, 128], P(('mob', 'imm')), may hold values from 0 to 4
- walk: float32 [2, 512, 3, 128], P(None, ('mob', 'imm')), may hold values from -1.8 to 1.8
- mobile_conc: float32 [512, 8, 128], P(('mob', 'imm')), may hold values from 0 to 2
- matrix_positions: float32 [512, 3, 128], P(('mob', 'imm')), may hold values from 0 to 4
- matrix_conc: float32 [512, 8, 128], P(('mob', 'imm')), may hold values from 0 to 2
- pair_rows: int32 [2, 16, 512], P('mob', 'imm'), may hold values from 0 to 255, as said below
- pair_cols: int32 [2, 16, 512], P('mob', 'imm'), may hold values from 0 to 31
- pair_counts: int32 [2, 16], P('mob', 'imm'), may hold values from 128 to 512, as said below
Outputs:
- mobile_after: float32 [512, 8, 128], P(('mob', 'imm'))
- matrix_after: float32 [512, 8, 128], P(('mob', 'imm'))
Inputs may be any that keep to these rules, and one draw needn't show every extreme that they name: Within one device the listed pairs (pair_rows, pair_cols) are distinct. `pair_counts`: in every draw some device uses all 512 slots.
All inputs are finite; a program needn't handle non-finite values.
Results may differ from a plain program's by a relative error of at most 0.0003.
Values sent between devices are 32-bit elements; how exact they have to be, the bound alone decides.
A program may use at most 64 MiB of HBM per device.

v0:
```python
import functools
import math

import jax
import jax.numpy as jnp
from jax import lax
from jax.experimental import pallas as pl
from jax.experimental.pallas import tpu as pltpu
from jax.sharding import PartitionSpec as P

RATE = 1.0 / 512.0
SCALE = math.sqrt(0.5 * math.log2(math.e))
CENTRE = 2.0
FAR = -30000.0
MESH = pl.DeviceIdType.MESH
VMEM_LIMIT = 20 * 1024 * 1024
UNROLL = 8
TERMS = 16
F32 = jnp.float32
BF16 = jnp.bfloat16


def sizes(n_mob, n_imm):
    rest = n_imm // 2
    nb = 1
    while nb * nb * 4 <= rest:
        nb *= 2
    return n_mob, nb, rest // nb


class Place:
    def __init__(self, n_mob, n_imm):
        self.nm, self.nb, self.na = sizes(n_mob, n_imm)
        self.p = lax.axis_index("mob")
        q = lax.axis_index("imm")
        self.core = lax.rem(q, 2)
        chip = lax.div(q, 2)
        self.b = lax.rem(chip, self.nb)
        self.a = lax.div(chip, self.nb)

    def am(self, d):
        return lax.rem(self.a + (d + self.na), self.na)

    def bm(self, d):
        return lax.rem(self.b + (d + self.nb), self.nb)

    def pm(self, d):
        return lax.rem(self.p + (d + self.nm), self.nm)

    def dev(self, p, a, b, core):
        return (p, (a * self.nb + b) * 2 + core)

    def along(self, da):
        return self.dev(self.p, self.am(da), self.b, self.core)

    def other(self, dc):
        return 1 - self.core if dc else self.core

    def across(self, dp, db, dc):
        return self.dev(self.pm(dp), self.a, self.bm(db), self.other(dc))

    def plane(self):
        keys = [(dp, db) for dp in range(self.nm) for db in range(self.nb)]
        return sorted((key for key in keys if any(key)), key=lambda key: -bool(key[0]) - bool(key[1]))

    def mates(self):
        return [(db, dc) for db in range(self.nb) for dc in range(2) if db or dc]

    def slot(self, dp, db, dc):
        return (self.pm(dp) * self.nb + self.bm(db)) * 2 + self.other(dc)

    def greet(self, lists=False):
        sem = pltpu.get_barrier_semaphore()
        peers = [self.along(d) for d in range(1, self.na)] + [self.across(0, 0, 1)]
        peers += [self.across(dp, db, 0) for dp, db in self.plane()]
        if lists:
            peers += [self.across(0, db, 1) for db in range(1, self.nb)]
        for peer in peers:
            pl.semaphore_signal(sem, inc=1, device_id=peer, device_id_type=MESH)
        return sem, len(peers)


def remote(src, dst, sems, index, device):
    copy = pltpu.make_async_remote_copy(
        src_ref=src, dst_ref=dst, send_sem=sems[0].at[index], recv_sem=sems[1].at[index],
        device_id=device, device_id_type=MESH,
    )
    copy.start()
    return copy


def split2(x):
    high = x.astype(BF16).astype(F32)
    return high, x - high


def split3(x):
    high, rest = split2(x)
    mid, low = split2(rest)
    return high, mid, low


def rows_x(x):
    (xh, xm), (yh, ym), (zh, zm) = [split2(x[j]) for j in range(3)]
    norm = split3(-(x[0] * x[0] + x[1] * x[1] + x[2] * x[2]))
    one = jnp.ones_like(x[0])
    return [xh, yh, zh, xh, yh, zh, xm, ym, zm, *norm, one, one, one, jnp.zeros_like(one)]


def rows_y(y):
    (xh, xm), (yh, ym), (zh, zm) = [split2(2.0 * y[j]) for j in range(3)]
    norm = split3(-(y[0] * y[0] + y[1] * y[1] + y[2] * y[2]))
    one = jnp.ones_like(y[0])
    return [xh, yh, zh, xm, ym, zm, xh, yh, zh, one, one, one, *norm, jnp.zeros_like(one)]


def fill(stage, rows):
    cells = rows[0].shape[0]
    for j, row in enumerate(rows):
        stage[pl.ds(j, cells, stride=TERMS), :] = row


def build_y(pos, stage, out, slot):
    cells = pos.shape[1]
    fill(stage, rows_y([pos[j] for j in range(3)]))
    out[pl.ds(slot * cells, cells)] = stage[...].reshape(cells, TERMS, 128).astype(BF16)


def build_x(pos, stage, out, slot):
    cells = pos.shape[1]
    fill(stage, rows_x([pos[j] for j in range(3)]))
    for group in range(0, cells, 128 // TERMS):
        block = stage[group * TERMS : group * TERMS + 128, :].T.astype(BF16)
        for j in range(128 // TERMS):
            out[slot * cells + group + j, :, :TERMS] = block[:, j * TERMS : (j + 1) * TERMS]


def count_list(at, mc, ic, lists, keep_m, keep_i, keep_rank, first, last, total):
    lists_n = lists.shape[0]
    cells_m = at.na * mc
    shift_m, shift_i, shift_b = [int(math.log2(n)) for n in (mc, ic, at.nb)]
    lane = lax.broadcasted_iota(jnp.int32, (1, 128), 1)
    mine = lax.broadcasted_iota(jnp.int32, (cells_m, 128), 0)
    upper = jnp.where(
        lax.broadcasted_iota(jnp.int32, (128, 128), 0) <= lax.broadcasted_iota(jnp.int32, (128, 128), 1), 1.0, 0.0
    ).astype(BF16)
    home = at.b * 2 + at.core

    def count(chunk, total):
        which, part = lax.rem(lax.div(chunk, 4) + home, lists_n), lax.rem(chunk, 4)
        r = lists[which, pl.ds(part, 1), :]
        c = lists[which, pl.ds(4 + part, 1), :]
        used = lists[which, 8:9, :]
        owner = jnp.right_shift(r, shift_m)
        ok = (
            (part * 128 + lane < used)
            & (jnp.bitwise_and(owner, 1) == at.core)
            & (jnp.bitwise_and(jnp.right_shift(owner, 1), at.nb - 1) == at.b)
        )
        m = jnp.right_shift(owner, 1 + shift_b) * mc + jnp.bitwise_and(r, mc - 1)
        m = jnp.where(ok, m, -1)
        i = (jnp.right_shift(c, shift_i) * lists_n + which) * ic + jnp.bitwise_and(c, ic - 1)
        hot = jnp.where(mine == m, 1.0, 0.0).astype(F32)
        rank = total + jnp.dot(hot.astype(BF16), upper, preferred_element_type=F32)
        keep_m[pl.ds(chunk, 1), :] = m
        keep_i[pl.ds(chunk, 1), :] = i + 1
        keep_rank[pl.ds(chunk, 1), :] = jnp.sum(hot * rank, axis=0, keepdims=True) - 1.0
        return jnp.broadcast_to(rank[:, 127:128], rank.shape)

    return lax.fori_loop(first, last, count, total, unroll=4)


def place_list(at, mc, ic, lists, keep_m, keep_i, keep_rank, total, out):
    lists_n, chunks = lists.shape[0], lists.shape[0] * 4
    cells_m = at.na * mc
    lines = -(-(out.shape[0] // 3) // 16) * 16
    mine = lax.broadcasted_iota(jnp.int32, (cells_m, 128), 0)
    lower = jnp.where(
        lax.broadcasted_iota(jnp.int32, (cells_m, cells_m), 0)
        > lax.broadcasted_iota(jnp.int32, (cells_m, cells_m), 1), 1.0, 0.0
    ).astype(F32)
    even = 2.0 * jnp.floor((total + 1.0) * 0.5)
    start = jnp.dot(lower, even, preferred_element_type=F32, precision=lax.Precision.HIGHEST)
    doubles = jnp.sum(even, axis=0, keepdims=True) * 0.5
    line = lax.broadcasted_iota(jnp.int32, (lines, 128), 0)
    column = lax.broadcasted_iota(jnp.int32, (128, 128), 0)

    def place(chunk, acc):
        m = keep_m[pl.ds(chunk, 1), :]
        i = keep_i[pl.ds(chunk, 1), :]
        hot = jnp.where(mine == m, 1.0, 0.0).astype(F32)
        spot = jnp.sum(hot * start, axis=0, keepdims=True) + keep_rank[pl.ds(chunk, 1), :]
        spot = jnp.where(m >= 0, spot.astype(jnp.int32), -1)
        double = jnp.right_shift(spot, 1)
        second = jnp.bitwise_and(spot, 1) == 1
        here = (line == jnp.right_shift(double, 7)) & (m >= 0)
        lane_hot = jnp.where(column == jnp.bitwise_and(double, 127), 1.0, 0.0).astype(BF16)
        high = jnp.right_shift(i, 6).astype(F32)
        low = jnp.bitwise_and(i, 63).astype(F32)
        zero = jnp.zeros((1, 128), F32)
        values = [
            jnp.where(second, zero, m.astype(F32)),
            jnp.where(second, zero, high),
            jnp.where(second, zero, low),
            jnp.where(second, high, zero),
            jnp.where(second, low, zero),
        ]
        left = jnp.concatenate([jnp.where(here, v, 0.0) for v in values], axis=0).astype(BF16)
        return acc + lax.dot_general(left, lane_hot, (((1,), (1,)), ((), ())), preferred_element_type=F32)

    acc = lax.fori_loop(0, chunks, place, jnp.zeros((5 * lines, 128), F32), unroll=4)
    m, high1, low1, high2, low2 = [
        acc[j * lines : (j + 1) * lines].astype(jnp.int32) for j in range(5)
    ]
    dummy = at.nm * lists_n * ic
    size = out.shape[0] // 3
    out[0:size, :] = m[0:size]
    for j, (high, low) in enumerate(((high1, low1), (high2, low2)), 1):
        i = (high * 64 + low)[0:size]
        out[j * size : (j + 1) * size, :] = jnp.where(i == 0, dummy, i - 1)
    out[out.shape[0] - 1 :, :] = doubles.astype(jnp.int32)


def conc_rows(conc):
    conc = conc * RATE
    high = conc.astype(BF16).astype(F32)
    ones = jnp.full_like(conc, RATE)
    return jnp.concatenate([high, conc - high, ones, ones], axis=1).astype(BF16)


def fill_rows(conc, rows, slot):
    cells = conc.shape[1]
    rows[pl.ds(slot * cells, cells)] = conc_rows(conc[slot])


def share_plane(at, src, dst, sems, pass_sems):
    me = at.slot(0, 0, 0)
    copies = {
        (dp, db): remote(src, dst.at[me], sems, (dp, db), at.across(dp, db, 0)) for dp, db in at.plane()
    }
    return copies, {(0, 0): remote(src, dst.at[me], pass_sems, (0, 0), at.across(0, 0, 1))}


def pass_on(at, copies, passed, dst, pass_sems):
    for (dp, db), copy in copies.items():
        copy.wait_recv()
        block = dst.at[at.slot(-dp, -db, 0)]
        passed[dp, db] = remote(block, block, pass_sems, (dp, db), at.across(0, 0, 1))


def share_along(at, src, dst, sems):
    return {da: remote(src, dst.at[at.a], sems, da, at.along(da)) for da in range(1, at.na)}


def take_plane(at, copies, passed, conc, rows):
    for dp, db in copies:
        fill_rows(conc, rows, at.slot(-dp, -db, 0))
    for (dp, db), copy in passed.items():
        copy.wait_recv()
        fill_rows(conc, rows, at.slot(-dp, -db, 1))


def take_along(at, copies, conc, rows):
    for da, copy in copies.items():
        copy.wait_recv()
        fill_rows(conc, rows, at.am(-da))


def finish_sends(*groups):
    for group in groups:
        for copy in group.values():
            copy.wait_send()


def first_gather(n_mob, n_imm, mpos, walk, mconc, ipos, iconc, rows, cols, count,
                 g_conc, h_conc, m_rows, i_rows, x_one, y_all, pair_list, x_two,
                 g_pos, h_pos, lists, in_m, in_w, in_i, in_r, in_c, in_n, stage, keep_m, keep_i, keep_rank, *sems):
    at = Place(n_mob, n_imm)
    local = sems[0]
    z_pos, z_conc, p_pos, p_conc, c_pos, c_conc, l_sem = [sems[j : j + 2] for j in range(1, 15, 2)]
    me = at.slot(0, 0, 0)
    reads = [
        pltpu.make_async_copy(src, dst, local.at[j])
        for j, (src, dst) in enumerate((
            (mpos, in_m), (walk, in_w), (ipos, in_i), (rows, in_r), (cols, in_c), (count, in_n),
            (mconc, g_conc.at[at.a]), (iconc, h_conc.at[me]),
        ))
    ]
    for read in reads:
        read.start()
    sem, peers = at.greet(lists=True)
    h_conc[h_conc.shape[0] - 1] = jnp.zeros(h_conc.shape[1:], F32)
    i_rows[i_rows.shape[0] - 16 :] = jnp.zeros((16,) + i_rows.shape[1:], BF16)
    cells_i = y_all.shape[0] - 8
    row = lax.broadcasted_iota(jnp.int32, (8, TERMS, 128), 1)
    y_all[cells_i:, :, :] = jnp.where(row == 12, FAR, 0.0).astype(BF16)
    reads[0].wait()
    reads[1].wait()
    moved = in_m[...] + in_w[0]
    g_pos[at.a] = (moved - CENTRE) * SCALE
    x_two[...] = ((moved + in_w[1]) - CENTRE) * SCALE
    reads[2].wait()
    h_pos[me] = (in_i[...] - CENTRE) * SCALE
    for read in reads[3:6]:
        read.wait()
    home = at.b * 2 + at.core
    for j in range(4):
        lists[home, j : j + 1, :] = in_r[0, :, j * 128 : (j + 1) * 128]
        lists[home, 4 + j : 5 + j, :] = in_c[0, :, j * 128 : (j + 1) * 128]
    lists[home, 8:16, :] = jnp.broadcast_to(in_n[...], (8, 128))
    build_x(g_pos.at[at.a], stage, x_one, at.a)
    build_y(h_pos.at[me], stage, y_all, me)
    for read in reads[6:]:
        read.wait()
    fill_rows(g_conc, m_rows, at.a)
    fill_rows(h_conc, i_rows, me)
    mc, ic = mconc.shape[0], iconc.shape[0]
    total = count_list(at, mc, ic, lists, keep_m, keep_i, keep_rank, 0, 4, jnp.zeros((at.na * mc, 128), F32))
    pl.semaphore_wait(sem, peers)
    z_far = share_along(at, g_pos.at[at.a], g_pos, z_pos)
    z_conc = share_along(at, g_conc.at[at.a], g_conc, z_conc)
    shared = {
        (db, dc): remote(lists.at[home], lists.at[home], l_sem, (db, dc), at.across(0, db, dc))
        for db, dc in at.mates()
    }
    p_far, p_near = share_plane(at, h_pos.at[me], h_pos, p_pos, c_pos)
    p_conc, p_near_conc = share_plane(at, h_conc.at[me], h_conc, p_conc, c_conc)
    for copy in shared.values():
        copy.wait_recv()
    total = count_list(at, mc, ic, lists, keep_m, keep_i, keep_rank, 4, lists.shape[0] * 4, total)
    place_list(at, mc, ic, lists, keep_m, keep_i, keep_rank, total, pair_list)
    pass_on(at, p_far, p_near, h_pos, c_pos)
    pass_on(at, p_conc, p_near_conc, h_conc, c_conc)
    for dp, db in p_far:
        here = at.slot(-dp, -db, 0)
        build_y(h_pos.at[here], stage, y_all, here)
    for (dp, db), copy in p_near.items():
        copy.wait_recv()
        here = at.slot(-dp, -db, 1)
        build_y(h_pos.at[here], stage, y_all, here)
    for da, copy in z_far.items():
        copy.wait_recv()
        build_x(g_pos.at[at.am(-da)], stage, x_one, at.am(-da))
    take_plane(at, p_conc, p_near_conc, h_conc, i_rows)
    take_along(at, z_conc, g_conc, m_rows)
    finish_sends(z_far, z_conc, shared, p_far, p_near, p_conc, p_near_conc)


def reduce_start(at, part_m, part_i, land_m, land_c, out_b, land_b, z_sem, c_sem, b_sem):
    mc, ic = land_m.shape[1], land_c.shape[2]
    c_copies = {
        (dp, db): remote(
            part_i.at[pl.ds(at.slot(dp, db, 1) * ic, ic)], land_c.at[dp, db], c_sem, (dp, db), at.across(0, 0, 1))
        for dp, db in at.plane() + [(0, 0)]
    }
    z_copies = {
        da: remote(part_m.at[pl.ds(at.am(da) * mc, mc)], land_m.at[da], z_sem, da, at.along(da))
        for da in range(1, at.na)
    }
    b_copies = {}
    for dp, db in at.plane():
        c_copies[dp, db].wait_recv()
        out_b[dp, db] = part_i[pl.ds(at.slot(dp, db, 0) * ic, ic)] + land_c[dp, db]
        b_copies[dp, db] = remote(out_b.at[dp, db], land_b.at[dp, db], b_sem, (dp, db), at.across(dp, db, 0))
    return z_copies, c_copies, b_copies


def reduce_end(base, part, slot, land, copies):
    cells = base.shape[0]
    total = base[...] + part[pl.ds(slot * cells, cells)]
    for key, copy in copies.items():
        copy.wait_recv()
        total = total + land[key]
    return total


def reduce_plane_end(at, base, part, land_c, land_b, c_copies, b_copies):
    c_copies[0, 0].wait_recv()
    return reduce_end(base, part, at.slot(0, 0, 0), land_b, b_copies) + land_c[0, 0]


def exchange(n_mob, n_imm, part_m, part_i, conc_m, conc_i, x_two, own_m, own_i, g_conc, h_conc, m_rows, i_rows,
             x_all, land_m, land_c, out_b, land_b, g_pos, stage, *sems):
    at = Place(n_mob, n_imm)
    z_sem, c_sem, b_sem, z_pos, z_conc, p_conc, c_conc = [sems[j : j + 2] for j in range(0, 14, 2)]
    sem, peers = at.greet()
    h_conc[h_conc.shape[0] - 1] = jnp.zeros(h_conc.shape[1:], F32)
    i_rows[i_rows.shape[0] - 16 :] = jnp.zeros((16,) + i_rows.shape[1:], BF16)
    pl.semaphore_wait(sem, peers)
    z_copies, c_copies, b_copies = reduce_start(
        at, part_m, part_i, land_m, land_c, out_b, land_b, z_sem, c_sem, b_sem)
    z_far = share_along(at, x_two, g_pos, z_pos)
    build_x(x_two, stage, x_all, at.a)
    me = at.slot(0, 0, 0)
    own_i[...] = reduce_plane_end(at, conc_i, part_i, land_c, land_b, c_copies, b_copies)
    p_conc, p_near = share_plane(at, own_i, h_conc, p_conc, c_conc)
    own_m[...] = reduce_end(conc_m, part_m, at.a, land_m, z_copies)
    z_conc = share_along(at, own_m, g_conc, z_conc)
    g_conc[at.a] = own_m[...]
    h_conc[me] = own_i[...]
    fill_rows(g_conc, m_rows, at.a)
    fill_rows(h_conc, i_rows, me)
    for da, copy in z_far.items():
        copy.wait_recv()
        build_x(g_pos.at[at.am(-da)], stage, x_all, at.am(-da))
    pass_on(at, p_conc, p_near, h_conc, c_conc)
    take_plane(at, p_conc, p_near, h_conc, i_rows)
    take_along(at, z_conc, g_conc, m_rows)
    finish_sends(z_copies, c_copies, b_copies, z_far, z_conc, p_conc, p_near)


def last_reduce(n_mob, n_imm, part_m, part_i, conc_m, conc_i, own_m, own_i, land_m, land_c, out_b, land_b, *sems):
    at = Place(n_mob, n_imm)
    sem, peers = at.greet()
    pl.semaphore_wait(sem, peers)
    z_copies, c_copies, b_copies = reduce_start(
        at, part_m, part_i, land_m, land_c, out_b, land_b, sems[0:2], sems[2:4], sems[4:6])
    own_i[...] = reduce_plane_end(at, conc_i, part_i, land_c, land_b, c_copies, b_copies)
    own_m[...] = reduce_end(conc_m, part_m, at.a, land_m, z_copies)
    finish_sends(z_copies, c_copies, b_copies)


def pair_loop(pair_list, x_all, y_all, x_conc, y_conc, m_rows, i_rows, gain_m, gain_i,
              lst, p_even, p_odd, w_even, w_odd, sem):
    read = pltpu.make_async_copy(pair_list, lst, sem)
    read.start()
    gain_m[...] = jnp.zeros_like(gain_m)
    gain_i[...] = jnp.zeros_like(gain_i)
    read.wait()
    size = lst.shape[0] // 3 // 128 * 128
    used = lst[lst.shape[0] - 128]

    def entry(block, u):
        spot = block * UNROLL
        return lst[spot + u], lst[spot + (size + u)], lst[spot + (2 * size + u)]

    def measure(block, u, powers):
        m, i, k = entry(block, u)
        right = jnp.concatenate([y_all[i], y_all[k]], axis=1)
        powers[u] = jnp.dot(x_all[m][:, :TERMS], right, preferred_element_type=F32)

    def weigh(u, powers, weights):
        weights[u] = jnp.exp2(powers[u]).astype(BF16)

    def transfer(block, u, weights):
        m, i, k = entry(block, u)
        weight = weights[u]
        to_i = jnp.dot(m_rows[m], weight, preferred_element_type=F32)
        right = jnp.concatenate([i_rows[i], i_rows[k]], axis=1)
        to_m = lax.dot_general(right, weight, (((1,), (1,)), ((), ())), preferred_element_type=F32)
        return m, i, k, to_i, to_m

    def finish(m, i, k, to_i, to_m):
        gain_m[m] += to_m[0:8] + to_m[8:16] - to_m[16:24] * x_conc[m]
        gain_i[i] += to_i[0:8, :128] + to_i[8:16, :128] - to_i[16:24, :128] * y_conc[i]
        gain_i[k] += to_i[0:8, 128:] + to_i[8:16, 128:] - to_i[16:24, 128:] * y_conc[k]

    def step(block, first=None, second=None, third=None):
        moved = []
        for u in range(UNROLL):
            if second is not None:
                weigh(u, *second)
            if first is not None:
                measure(block, u, first)
            if third is not None:
                moved.append(transfer(block - 2, u, third))
        for item in moved:
            finish(*item)

    pairs = jnp.maximum(lax.div(used + (2 * UNROLL - 1), 2 * UNROLL), 1)
    step(0, p_even)
    step(1, p_odd, (p_even, w_even))

    def body(t, carry):
        step(2 * t, p_even, (p_odd, w_odd), w_even)
        step(2 * t + 1, p_odd, (p_even, w_even), w_odd)
        return carry

    lax.fori_loop(1, pairs, body, 0)
    step(2 * pairs, None, (p_odd, w_odd), w_even)
    step(2 * pairs + 1, None, None, w_odd)


def on_device(n_mob, n_imm, mpos, walk, mconc, ipos, iconc, rows, cols, counts):
    nm, nb, na = sizes(n_mob, n_imm)
    mc, solutes, part = mconc.shape
    ic = iconc.shape[0]
    slots = nm * nb * 2
    cells_m, cells_i = na * mc, slots * ic
    tiles = nb * 2
    chunks = tiles * 4
    lines = -(-(chunks * 64 + cells_m // 2 + 2 * UNROLL) // 128)
    list_rows = -(-(3 * lines + 1) // 8) * 8
    vmem = pl.BlockSpec(memory_space=pltpu.VMEM)
    anywhere = pl.BlockSpec(memory_space=pl.ANY)
    hbm = pl.BlockSpec(memory_space=pltpu.HBM)
    dma = pltpu.SemaphoreType.DMA

    def params(ident):
        return pltpu.CompilerParams(collective_id=ident, has_side_effects=True, vmem_limit_bytes=VMEM_LIMIT)

    def shape(dims, dtype=F32):
        return jax.ShapeDtypeStruct(dims, dtype)

    def pairs(*dims):
        return [dma(dims)] * 2

    cell_m, cell_i = (mc, solutes, part), (ic, solutes, part)
    all_m, all_i = (na,) + cell_m, (slots + 1,) + cell_i
    pos_m, pos_i = (3, mc, part), (3, ic, part)
    stage = pltpu.VMEM((max(mc, ic) * TERMS, part), F32)
    x_shape = shape((cells_m, part, 128), BF16)
    concs = (
        shape(all_m), shape(all_i),
        shape((cells_m, 4 * solutes, part), BF16), shape((cells_i + 16, 4 * solutes, part), BF16),
    )
    plane = (nm, nb)
    *concs_one, x_one, y_all, pair_list, x_two = pl.pallas_call(
        functools.partial(first_gather, n_mob, n_imm),
        out_shape=concs + (
            x_shape, shape((cells_i + 8, TERMS, part), BF16), shape((list_rows, 128), jnp.int32), shape(pos_m),
        ),
        in_specs=[hbm] * 8,
        out_specs=(vmem,) * 8,
        scratch_shapes=[
            pltpu.VMEM((na,) + pos_m, F32), pltpu.VMEM((slots,) + pos_i, F32),
            pltpu.VMEM((tiles, 16, 128), jnp.int32),
            pltpu.VMEM(pos_m, F32), pltpu.VMEM((2,) + pos_m, F32), pltpu.VMEM(pos_i, F32),
            pltpu.VMEM(rows.shape, jnp.int32), pltpu.VMEM(cols.shape, jnp.int32), pltpu.VMEM((1, 1), jnp.int32),
            stage, pltpu.VMEM((chunks, 128), jnp.int32), pltpu.VMEM((chunks, 128), jnp.int32),
            pltpu.VMEM((chunks, 128), F32),
            dma((8,)), *pairs(na), *pairs(na), *pairs(*plane), *pairs(*plane), *pairs(*plane), *pairs(*plane),
            *pairs(nb, 2),
        ],
        compiler_params=params(0),
    )(*[
        pltpu.with_memory_space_constraint(x, pltpu.HBM)
        for x in (jnp.transpose(mpos, (1, 0, 2)), jnp.transpose(walk, (0, 2, 1, 3)), mconc,
                  jnp.transpose(ipos, (1, 0, 2)), iconc, rows, cols)
    ], counts)
    flat_list = pair_list.reshape(-1)

    def gains(x_all, x_conc, y_conc, m_rows, i_rows):
        return pl.pallas_call(
            pair_loop,
            out_shape=(shape((cells_m, solutes, part)), shape((cells_i + 1, solutes, part))),
            in_specs=[anywhere] + [vmem] * 6,
            out_specs=(vmem,) * 2,
            scratch_shapes=[
                pltpu.SMEM((flat_list.shape[0],), jnp.int32),
                pltpu.VMEM((UNROLL, part, 256), F32), pltpu.VMEM((UNROLL, part, 256), F32),
                pltpu.VMEM((UNROLL, part, 256), BF16), pltpu.VMEM((UNROLL, part, 256), BF16),
                dma,
            ],
            compiler_params=pltpu.CompilerParams(vmem_limit_bytes=VMEM_LIMIT),
        )(flat_list, x_all, y_all, x_conc.reshape((cells_m, solutes, part)),
          y_conc.reshape((cells_i + ic, solutes, part)), m_rows, i_rows)

    lands = [pltpu.VMEM((na,) + cell_m, F32)] + [pltpu.VMEM(plane + cell_i, F32)] * 3
    own = (shape(cell_m), shape(cell_i))
    part_m, part_i = gains(x_one, *concs_one)
    own_m, own_i, *concs_two, x_all = pl.pallas_call(
        functools.partial(exchange, n_mob, n_imm),
        out_shape=own + concs + (x_shape,),
        in_specs=[vmem] * 5,
        out_specs=(vmem,) * 7,
        scratch_shapes=lands + [pltpu.VMEM((na,) + pos_m, F32), stage, *pairs(na), *pairs(*plane), *pairs(*plane),
                                *pairs(na), *pairs(na), *pairs(*plane), *pairs(*plane)],
        compiler_params=params(1),
    )(part_m, part_i, mconc, iconc, x_two)
    part_m, part_i = gains(x_all, *concs_two)
    return pl.pallas_call(
        functools.partial(last_reduce, n_mob, n_imm),
        out_shape=own,
        in_specs=[vmem] * 4,
        out_specs=(vmem,) * 2,
        scratch_shapes=lands + [*pairs(na), *pairs(*plane), *pairs(*plane)],
        compiler_params=params(2),
    )(part_m, part_i, own_m, own_i)


def solution(mesh):
    return jax.shard_map(
        functools.partial(on_device, mesh.shape["mob"], mesh.shape["imm"]),
        mesh=mesh,
        in_specs=(
            P(("mob", "imm"), None, None),
            P(None, ("mob", "imm"), None, None),
            P(("mob", "imm"), None, None),
            P(("mob", "imm"), None, None),
            P(("mob", "imm"), None, None),
            P("mob", "imm", None),
            P("mob", "imm", None),
            P("mob", "imm"),
        ),
        out_specs=(P(("mob", "imm"), None, None), P(("mob", "imm"), None, None)),
        check_vma=False,
    )
```

profile of v0, /device:TPU:0, one launch (start us, length us, event | category | flops | bytes accessed | tf_op | source)
XLA Modules:
  0.0 61.1 jit_solution(15364883280592440597)
XLA Ops:
  1.3 15.0 %shard_map.95 = (f32[4,16,8,128]{3,2,1,0:T(8,128)S(1)}, f32[9,16,8,128]{3,2,1,0:T(8,128)S(1)}, bf16[64,32,128]{2,1,0:T(8,128)(2,1)S(1)}, bf16[144,32,128]{2,1,0:...) custom-call(f32[3,16,128]{2,1,0:T(8,128)} %bitcast.15, ...), custom_call_target="tpu_custom_call" | custom-call | tf_op jit(solution)/shard_map/pallas_call | solution.py:518
  16.3 0.0 copy-start
  16.3 0.0 copy-start.1
  16.3 7.6 %shard_map.96 = (f32[64,8,128]{2,1,0:T(8,128)S(1)}, f32[129,8,128]{2,1,0:T(8,128)S(1)}) custom-call(s32[4096]{0:T(1024)S(1)} %bitcast.12, bf16[64,128,128]{2,1,0:T(8,128)(2,1)S(1)} %get-tuple-element.22.x_all, bf16[136,16,128]{2,1,0:T(8,128)(2,1)S(1)} %get-tuple-element.23.y_all, f32[64,8,128]{2,1,0:T(8,128)S(1)} %bitcast.11, f32[144,8,128]{2,1,0:T(8,128)S(1)} %bitcast.9, ...), custom_call_target="tpu_custom_call" | custom-call | tf_op jit(solution)/shard_map/pallas_call | solution.py:544
  23.9 0.0 copy-done
  23.9 0.0 copy-done.1
  23.9 17.2 %shard_map.97 = (f32[16,8,128]{2,1,0:T(8,128)S(1)}, f32[16,8,128]{2,1,0:T(8,128)S(1)}, f32[4,16,8,128]{3,2,1,0:T(8,128)S(1)}, f32[9,16,8,128]{3,2,1,0:T(8,128)S(...) custom-call(f32[64,8,128]{2,1,0:T(8,128)S(1)} %get-tuple-element.28.part_, ...), custom_call_target="tpu_custom_call" | custom-call | tf_op jit(solution)/shard_map/pallas_call | solution.py:562
  41.1 7.6 %shard_map.98 = (f32[64,8,128]{2,1,0:T(8,128)S(1)}, f32[129,8,128]{2,1,0:T(8,128)S(1)}) custom-call(s32[4096]{0:T(1024)S(1)} %bitcast.13, bf16[64,128,128]{2,1,0:T(8,128)(2,1)S(1)} %get-tuple-element.31.x_all, bf16[136,16,128]{2,1,0:T(8,128)(2,1)S(1)} %get-tuple-element.23.y_all, f32[64,8,128]{2,1,0:T(8,128)S(1)} %bitcast.10, f32[144,8,128]{2,1,0:T(8,128)S(1)} %bitcast.8, ...), custom_call_target="tpu_custom_call" | custom-call | tf_op jit(solution)/shard_map/pallas_call | solution.py:544
  48.7 11.1 %shard_map.99 = (f32[16,8,128]{2,1,0:T(8,128)S(1)}, f32[16,8,128]{2,1,0:T(8,128)S(1)}) custom-call(f32[64,8,128]{2,1,0:T(8,128)S(1)} %get-tuple-element.36.part_m, f32[129,8,128]{2,1,0:T(8,128)S(1)} %get-tuple-element.37.part_i, f32[16,8,128]{2,1,0:T(8,128)S(1)} %get-tuple-element.38.conc_m, f32[16,8,128]{2,1,0:T(8,128)S(1)} %get-tuple-element.39.conc_i), custom_call_target="tpu_custom_call" | custom-call | tf_op jit(solution)/shard_map/pallas_call | solution.py:572
  59.9 0.6 %copy.13 = f32[16,8,128]{2,1,0:T(8,128)} copy(f32[16,8,128]{2,1,0:T(8,128)S(1)} %get-tuple-element.42) | data formatting | bytes 131072
  60.5 0.6 %copy.14 = f32[16,8,128]{2,1,0:T(8,128)} copy(f32[16,8,128]{2,1,0:T(8,128)S(1)} %get-tuple-element.43) | data formatting | bytes 131072
Async XLA Ops:
  16.3 7.6 %copy-start = (f32[16,8,128]{2,1,0:T(8,128)S(1)}, f32[16,8,128]{2,1,0:T(8,128)}, u32[]{:S(2)}) copy-start(f32[16,8,128]{2,1,0:T(8,128)} %conc_m.1) | copy-start | bytes 196612
  16.3 7.6 %copy-start.1 = (f32[16,8,128]{2,1,0:T(8,128)S(1)}, f32[16,8,128]{2,1,0:T(8,128)}, u32[]{:S(2)}) copy-start(f32[16,8,128]{2,1,0:T(8,128)} %conc_i.1) | copy-start | bytes 196612
where the time goes:
time: 61.3 us; the launch traced here: 61.1 us
  Pallas kernels  58.5 us (95%)
  between operations  1.35 us (2%)
  local copies, waits for them, and re-layouts  1.27 us (2%)
    pallas_call x1, Pallas kernels, on_device(): pl.pallas_call(functools.partial(exchange, n_mob, n_imm), out_shape=own +...  17.2 us
    pallas_call x2, Pallas kernels, gains(): pl.pallas_call(pair_loop, out_shape=(shape((cells_m, solutes, part)), sha...  15.2 us
    pallas_call x1, Pallas kernels, on_device(): pl.pallas_call(functools.partial(first_gather, n_mob, n_imm), out_shape=c...  15 us
    pallas_call x1, Pallas kernels, on_device(): pl.pallas_call(functools.partial(last_reduce, n_mob, n_imm), out_shape=ow...  11.1 us
    unnamed x6, local copies, waits for them, and re-layouts  1.27 us

commit v1 on v0

--- a/solution.py
+++ b/solution.py
@@ -14,7 +14,7 @@
 FAR = -30000.0
 MESH = pl.DeviceIdType.MESH
 VMEM_LIMIT = 20 * 1024 * 1024
-UNROLL = 8
+UNROLL = 16
 TERMS = 16
 F32 = jnp.float32
 BF16 = jnp.bfloat16
@@ -481,6 +481,16 @@
     step(2 * pairs + 1, None, None, w_odd)
 
 
+def write_out(own_m, own_i, out_m, out_i, sems):
+    copies = [
+        pltpu.make_async_copy(src, dst, sems.at[j]) for j, (src, dst) in enumerate(((own_m, out_m), (own_i, out_i)))
+    ]
+    for copy in copies:
+        copy.start()
+    for copy in copies:
+        copy.wait()
+
+
 def on_device(n_mob, n_imm, mpos, walk, mconc, ipos, iconc, rows, cols, counts):
     nm, nb, na = sizes(n_mob, n_imm)
     mc, solutes, part = mconc.shape
@@ -569,7 +579,7 @@
         compiler_params=params(1),
     )(part_m, part_i, mconc, iconc, x_two)
     part_m, part_i = gains(x_all, *concs_two)
-    return pl.pallas_call(
+    own_m, own_i = pl.pallas_call(
         functools.partial(last_reduce, n_mob, n_imm),
         out_shape=own,
         in_specs=[vmem] * 4,
@@ -577,6 +587,14 @@
         scratch_shapes=lands + [*pairs(na), *pairs(*plane), *pairs(*plane)],
         compiler_params=params(2),
     )(part_m, part_i, own_m, own_i)
+    return pl.pallas_call(
+        write_out,
+        out_shape=own,
+        in_specs=[vmem] * 2,
+        out_specs=(anywhere,) * 2,
+        scratch_shapes=[dma((2,))],
+        compiler_params=pltpu.CompilerParams(vmem_limit_bytes=VMEM_LIMIT),
+    )(own_m, own_i)
 
 
 def solution(mesh):

time: 61.3 us -> 58.6 us (0.956)
  Pallas kernels: 58.5 us -> 56.4 us
  local copies, waits for them, and re-layouts: 1.27 us -> 0.01 us
    unnamed x6 -> x4, local copies, waits for them, and re-layouts: 1.27 us -> 0.01 us
    pallas_call x1, Pallas kernels: 11.1 us -> 9.96 us  [on_device(): pl.pallas_call(functools.partial(last_reduce, n_mob, n_imm), out_shape=ow...]
    pallas_call x1, Pallas kernels: 17.2 us -> 16.4 us  [on_device(): pl.pallas_call(functools.partial(exchange, n_mob, n_imm), out_shape=own +...]
    pallas_call x2, Pallas kernels: 15.2 us -> 14.5 us  [gains(): pl.pallas_call(pair_loop, out_shape=(shape((cells_m, solutes, part)), sha...]
    pallas_call x0 -> x1, Pallas kernels: none -> 0.67 us  [on_device(): pl.pallas_call(write_out, out_shape=own, in_specs=[vmem] * 2, out_specs=(...]
where the time goes in v1:
time: 58.6 us; the launch traced here: 57.8 us
  Pallas kernels  56.4 us (96%)
  between operations  1.35 us (2%)
    pallas_call x1, Pallas kernels, on_device(): pl.pallas_call(functools.partial(exchange, n_mob, n_imm), out_shape=own +...  16.4 us
    pallas_call x1, Pallas kernels, on_device(): pl.pallas_call(functools.partial(first_gather, n_mob, n_imm), out_shape=c...  15 us
    pallas_call x2, Pallas kernels, gains(): pl.pallas_call(pair_loop, out_shape=(shape((cells_m, solutes, part)), sha...  14.5 us
    pallas_call x1, Pallas kernels, on_device(): pl.pallas_call(functools.partial(last_reduce, n_mob, n_imm), out_shape=ow...  9.96 us

profile of v1, /device:TPU:0, one launch (start us, length us, event | category | flops | bytes accessed | tf_op | source)
XLA Modules:
  0.0 57.8 jit_solution(8222295949308465819)
XLA Ops:
  1.3 15.0 %shard_map.95 = (f32[4,16,8,128]{3,2,1,0:T(8,128)S(1)}, f32[9,16,8,128]{3,2,1,0:T(8,128)S(1)}, bf16[64,32,128]{2,1,0:T(8,128)(2,1)S(1)}, bf16[144,32,128]{2,1,0:...) custom-call(f32[3,16,128]{2,1,0:T(8,128)} %bitcast.15, ...), custom_call_target="tpu_custom_call" | custom-call | tf_op jit(solution)/shard_map/pallas_call | solution.py:528
  16.3 0.0 copy-start
  16.3 0.0 copy-start.1
  16.3 7.2 %shard_map.96 = (f32[64,8,128]{2,1,0:T(8,128)S(1)}, f32[129,8,128]{2,1,0:T(8,128)S(1)}) custom-call(s32[4096]{0:T(1024)S(1)} %bitcast.12, bf16[64,128,128]{2,1,0:T(8,128)(2,1)S(1)} %get-tuple-element.24.x_all, bf16[136,16,128]{2,1,0:T(8,128)(2,1)S(1)} %get-tuple-element.25.y_all, f32[64,8,128]{2,1,0:T(8,128)S(1)} %bitcast.11, f32[144,8,128]{2,1,0:T(8,128)S(1)} %bitcast.9, ...), custom_call_target="tpu_custom_call" | custom-call | tf_op jit(solution)/shard_map/pallas_call | solution.py:554
  23.5 0.0 copy-done
  23.5 0.0 copy-done.1
  23.5 16.4 %shard_map.97 = (f32[16,8,128]{2,1,0:T(8,128)S(1)}, f32[16,8,128]{2,1,0:T(8,128)S(1)}, f32[4,16,8,128]{3,2,1,0:T(8,128)S(1)}, f32[9,16,8,128]{3,2,1,0:T(8,128)S(...) custom-call(f32[64,8,128]{2,1,0:T(8,128)S(1)} %get-tuple-element.30.part_, ...), custom_call_target="tpu_custom_call" | custom-call | tf_op jit(solution)/shard_map/pallas_call | solution.py:572
  39.9 7.3 %shard_map.98 = (f32[64,8,128]{2,1,0:T(8,128)S(1)}, f32[129,8,128]{2,1,0:T(8,128)S(1)}) custom-call(s32[4096]{0:T(1024)S(1)} %bitcast.13, bf16[64,128,128]{2,1,0:T(8,128)(2,1)S(1)} %get-tuple-element.33.x_all, bf16[136,16,128]{2,1,0:T(8,128)(2,1)S(1)} %get-tuple-element.25.y_all, f32[64,8,128]{2,1,0:T(8,128)S(1)} %bitcast.10, f32[144,8,128]{2,1,0:T(8,128)S(1)} %bitcast.8, ...), custom_call_target="tpu_custom_call" | custom-call | tf_op jit(solution)/shard_map/pallas_call | solution.py:554
  47.2 10.0 %shard_map.99 = (f32[16,8,128]{2,1,0:T(8,128)S(1)}, f32[16,8,128]{2,1,0:T(8,128)S(1)}) custom-call(f32[64,8,128]{2,1,0:T(8,128)S(1)} %get-tuple-element.38.part_m, f32[129,8,128]{2,1,0:T(8,128)S(1)} %get-tuple-element.39.part_i, f32[16,8,128]{2,1,0:T(8,128)S(1)} %get-tuple-element.40.conc_m, f32[16,8,128]{2,1,0:T(8,128)S(1)} %get-tuple-element.41.conc_i), custom_call_target="tpu_custom_call" | custom-call | tf_op jit(solution)/shard_map/pallas_call | solution.py:582
  57.1 0.7 %shard_map.100 = (f32[16,8,128]{2,1,0:T(8,128)}, f32[16,8,128]{2,1,0:T(8,128)}) custom-call(f32[16,8,128]{2,1,0:T(8,128)S(1)} %get-tuple-element.42.own_m, f32[16,8,128]{2,1,0:T(8,128)S(1)} %get-tuple-element.43.own_i), custom_call_target="tpu_custom_call" | custom-call | tf_op jit(solution)/shard_map/pallas_call | solution.py:590
Async XLA Ops:
  16.3 7.2 %copy-start = (f32[16,8,128]{2,1,0:T(8,128)S(1)}, f32[16,8,128]{2,1,0:T(8,128)}, u32[]{:S(2)}) copy-start(f32[16,8,128]{2,1,0:T(8,128)} %conc_m.1) | copy-start | bytes 196612
  16.3 7.2 %copy-start.1 = (f32[16,8,128]{2,1,0:T(8,128)S(1)}, f32[16,8,128]{2,1,0:T(8,128)}, u32[]{:S(2)}) copy-start(f32[16,8,128]{2,1,0:T(8,128)} %conc_i.1) | copy-start | bytes 196612
